TPU v7x, 32 devices: a whole 2x2x4 slice. The times are simulated.
32 devices in a mesh: rows: 8 (over z, y), snaps: 4 (over x, core).
Axes of the slice: x: 2, y: 2, z: 4, core: 2. Of those that a mesh axis runs over, the one named last changes fastest.
Arguments:
- stress: float32 [131072, 1024], P('rows', 'snaps'), may hold values from -80 to 80
- sketch: float32 [64, 1024], P(None, 'snaps'), may hold values from -0.1875 to 0.1875
Outputs:
- basis: float32 [64, 131072], P(None, ('rows', 'snaps'))
- coeffs: float32 [64, 1024], P(None, 'snaps')
- spectrum: float32 [64, 64], replicated
All inputs are finite; a program needn't handle non-finite values.
Results may differ from a plain program's by a relative error of at most 0.0015.
Values sent between devices are 32-bit elements; how exact they have to be, the bound alone decides.
A program may use at most 128 MiB of HBM per device.

v0:
```python
import functools
import math

import jax
import jax.numpy as jnp
from jax import lax
from jax.experimental import pallas as pl
from jax.experimental.pallas import tpu as pltpu
from jax.sharding import PartitionSpec as P

MESH = pl.DeviceIdType.MESH
F32 = jnp.float32
BF16 = jnp.bfloat16
CHUNK = 1024
HALF = CHUNK // 2
SLOTS = 4
PIECE = 128
TURNS = 2


def dot(left_m, right_m, left_dim, right_dim, precision=None):
    return lax.dot_general(
        left_m,
        right_m,
        (((left_dim,), (right_dim,)), ((), ())),
        precision=precision,
        preferred_element_type=F32,
    )


def dot_full(left_m, right_m, left_dim, right_dim):
    return dot(left_m, right_m, left_dim, right_dim, lax.Precision.HIGHEST)


def split(value):
    high = value.astype(BF16)
    low = (value - high.astype(F32)).astype(BF16)
    return high, low


def inverse_factor(gram):
    k = gram.shape[0]
    line = lax.broadcasted_iota(jnp.int32, (k, k), 0)
    lane = lax.broadcasted_iota(jnp.int32, (k, k), 1)
    wide_line = lax.broadcasted_iota(jnp.int32, (k, 2 * k), 0)
    ident = jnp.where(line == lane, 1.0, 0.0).astype(F32)
    table = jnp.concatenate([gram, ident], axis=1)
    for j in range(k - 1):
        row = table[j : j + 1, :]
        row = row / row[:, j : j + 1]
        column = jnp.where(wide_line > j, table[:, j : j + 1], 0.0)
        table = table - column * row
    diag = jnp.sum(jnp.where(line == lane, table[:, :k], 0.0), axis=1, keepdims=True)
    return table[:, k:] / jnp.sqrt(diag)


def kernel(
    ranks, batch_total,
    stress, sketch, share_out, factor_out, coeffs_out, spectrum_out,
    stage, high, low, operand, part, got1, summed, got2, panel,
    acc, spread, landed, total, full, spect, gram, grams, acc_gram, factor, whole,
    stage_sem, share_sem, send1, recv1, send2, recv2, send3, recv3,
    rs_send, rs_recv, ag_send, ag_recv, sp_send, sp_recv, gr_send, gr_recv,
):
    groups = 4
    k = sketch.shape[0]
    width = stress.shape[1]
    chunks = part.shape[0]
    lines = k // ranks
    me_row = lax.axis_index("rows")
    me = lax.axis_index("snaps")
    mine = me % 2
    core = me + 1 - 2 * mine
    chip = (me + 2) % groups

    def load(c):
        slot = c % SLOTS
        return pltpu.make_async_copy(
            stress.at[pl.ds(c * CHUNK, CHUNK), :], stage.at[slot], stage_sem.at[slot]
        )

    for c in range(SLOTS):
        load(c).start()

    barrier = pltpu.get_barrier_semaphore()
    for d in range(1, ranks):
        pl.semaphore_signal(
            barrier, inc=1, device_id={"rows": (me_row + d) % ranks}, device_id_type=MESH
        )
    for d in range(1, groups):
        pl.semaphore_signal(
            barrier, inc=1, device_id={"snaps": (me + d) % groups}, device_id_type=MESH
        )

    def remote(src, dst, s_sem, r_sem, device):
        return pltpu.make_async_remote_copy(
            src_ref=src, dst_ref=dst, send_sem=s_sem, recv_sem=r_sem,
            device_id=device, device_id_type=MESH,
        )

    def hop1(t, c):
        return remote(
            part.at[c, 1 - mine], got1.at[t, c], send1.at[t, c], recv1.at[t, c], {"snaps": core}
        )

    def hop2(t, c):
        return remote(summed.at[c], got2.at[t, c], send2.at[t, c], recv2.at[t, c], {"snaps": chip})

    def hop3(t, c):
        return remote(
            panel.at[t, c, mine], panel.at[t, c, mine], send3.at[t, c], recv3.at[t, c],
            {"snaps": core},
        )

    def scatter(t, d):
        to = (me_row + d) % ranks
        return remote(
            spread.at[to], landed.at[t, d], rs_send.at[t, d], rs_recv.at[t, d], {"rows": to}
        )

    def gather(t, d):
        to = (me_row + d) % ranks
        return remote(
            total.at[t], full.at[t, me_row], ag_send.at[t, d], ag_recv.at[t, d], {"rows": to}
        )

    def give_gram(d):
        return remote(
            gram, grams.at[me_row], gr_send.at[d], gr_recv.at[d], {"rows": (me_row + d) % ranks}
        )

    def share_spectrum(d):
        return remote(
            spect.at[0], spect.at[d], sp_send.at[d], sp_recv.at[d], {"snaps": (me + d) % groups}
        )

    def share_copy():
        per = chunks // groups
        return pltpu.make_async_copy(whole.at[pl.ds(me * per, per)], share_out, share_sem)

    def set_operand(value):
        h, l = split(value)
        operand[0:k, :] = h
        operand[k : 2 * k, :] = l

    def convert(c):
        slot = c % SLOTS
        load(c).wait()

        def body(p, carry):
            h, l = split(stage[slot, pl.ds(p * PIECE, PIECE), :])
            at = pl.ds(c * CHUNK + p * PIECE, PIECE)
            high[at, :] = h
            low[at, :] = l
            return carry

        lax.fori_loop(0, CHUNK // PIECE, body, 0)

        @pl.when(c + SLOTS < chunks)
        def _():
            load(c + SLOTS).start()

    def project(t, c):
        if t == 0:
            convert(c)
        for h in range(2):
            at = pl.ds(c * CHUNK + h * HALF, HALF)
            both = dot(operand[...], high[at, :], 1, 1)
            rest = dot(operand[0:k, :], low[at, :], 1, 1)
            part[c, h] = both[0:k] + (both[k : 2 * k] + rest)

    def add_cores(t, c):
        hop1(t, c).wait_recv()
        summed[c] = part[c, mine] + got1[t, c]
        hop2(t, c).start()

    def add_chips(t, c):
        hop2(t, c).wait_recv()
        panel[t, c, mine] = summed[c] + got2[t, c]
        hop3(t, c).start()

    def accumulate(t, c):
        hop3(t, c).wait_recv()
        for h in range(2):
            value = panel[t, c, h]
            if t > 0:
                value = dot_full(factor[...], value, 1, 0)
                whole[c, h] = value
            hi, lo = split(value)
            at = pl.ds(c * CHUNK + h * HALF, HALF)
            both = dot(jnp.concatenate([hi, lo], axis=0), high[at, :], 1, 0)
            rest = dot(hi, low[at, :], 1, 0)
            acc[:, 0:width] += both[0:k] + (both[k : 2 * k] + rest)
            acc[:, width : width + k] += dot_full(value, value, 1, 1)

    set_operand(sketch[...])
    for t in range(TURNS):
        acc[...] = jnp.zeros_like(acc)
        project(t, 0)
        if t == 0:
            pl.semaphore_wait(barrier, ranks - 1 + groups - 1)
        hop1(t, 0).start()

        def first(c, carry, t=t):
            project(t, c)
            hop1(t, c).start()
            add_cores(t, c - 1)
            return carry

        lax.fori_loop(1, chunks, first, 0)
        add_cores(t, chunks - 1)
        if t > 0:
            factor[...] = inverse_factor(acc_gram[...])
        add_chips(t, 0)

        def second(c, carry, t=t):
            add_chips(t, c)
            accumulate(t, c - 1)
            return carry

        lax.fori_loop(1, chunks, second, 0)
        accumulate(t, chunks - 1)

        last = t == TURNS - 1
        if last:
            own_gram = acc[:, width : width + k]
            gram[...] = own_gram
            grams[me_row] = own_gram
            for d in range(1, ranks):
                give_gram(d).start()
        for r in range(ranks):
            spread[r] = acc[r * lines : (r + 1) * lines, :]
        for d in range(1, ranks):
            scatter(t, d).start()
        if last:
            for d in range(1, ranks):
                give_gram(d).wait_recv()
            gram_total = grams[0]
            for r in range(1, ranks):
                gram_total = gram_total + grams[r]
        value = spread[me_row]
        for d in range(1, ranks):
            scatter(t, d).wait_recv()
            value = value + landed[t, d]
        total[t] = value
        full[t, me_row] = value
        for d in range(1, ranks):
            gather(t, d).start()
        if last:
            share_copy().start()
            final = inverse_factor(gram_total)

        def drain(c, carry, t=t):
            hop1(t, c).wait_send()
            hop2(t, c).wait_send()
            hop3(t, c).wait_send()
            return carry

        lax.fori_loop(0, chunks, drain, 0)
        for d in range(1, ranks):
            scatter(t, d).wait_send()
        for d in range(1, ranks):
            gather(t, d).wait_recv()
        for r in range(ranks):
            acc[r * lines : (r + 1) * lines, :] = full[t, r]
        if not last:
            set_operand(acc[:, 0:width])
            acc_gram[...] = acc[:, width : width + k]

    sums = dot_full(final, acc[:, 0:width], 1, 0)
    coeffs_out[...] = sums
    factor_out[...] = final
    spect[0] = dot_full(sums, sums, 1, 1)
    for d in range(1, groups):
        share_spectrum(d).start()

    for d in range(1, ranks):
        give_gram(d).wait_send()
        for t in range(TURNS):
            gather(t, d).wait_send()
    share_copy().wait()
    for d in range(1, groups):
        share_spectrum(d).wait()
    a = spect[0] + spect[2]
    b = spect[1] + spect[3]
    spectrum_out[...] = (a + b) / batch_total


def finish(scale, factor, share, coeffs, spectrum, basis_out, coeffs_out, spectrum_out):
    scaled = factor[...] * scale
    for h in range(2):
        basis_out[:, h * HALF : (h + 1) * HALF] = dot_full(scaled, share[0, h], 1, 0)
    coeffs_out[...] = coeffs[...]
    spectrum_out[...] = spectrum[...]


def on_device(stress, sketch):
    rows_dev, width = stress.shape
    k = sketch.shape[0]
    groups = lax.axis_size("snaps")
    ranks = lax.axis_size("rows")
    share = rows_dev // groups
    chunks = rows_dev // CHUNK
    lines = k // ranks
    wide = width + 128
    scale = math.sqrt(float(rows_dev * ranks))
    vmem = pl.BlockSpec(memory_space=pltpu.VMEM)
    dma = pltpu.SemaphoreType.DMA
    per = chunks // groups
    part_out, factor, coeffs, spectrum = pl.pallas_call(
        functools.partial(kernel, ranks, float(width * groups)),
        out_shape=(
            jax.ShapeDtypeStruct((per, 2, k, HALF), F32),
            jax.ShapeDtypeStruct((k, k), F32),
            jax.ShapeDtypeStruct((k, width), F32),
            jax.ShapeDtypeStruct((k, k), F32),
        ),
        in_specs=[pl.BlockSpec(memory_space=pl.ANY), vmem],
        out_specs=(pl.BlockSpec(memory_space=pl.ANY), vmem, vmem, vmem),
        scratch_shapes=[
            pltpu.VMEM((SLOTS, CHUNK, width), F32),
            pltpu.VMEM((rows_dev, width), BF16),
            pltpu.VMEM((rows_dev, width), BF16),
            pltpu.VMEM((2 * k, width), BF16),
            pltpu.VMEM((chunks, 2, k, HALF), F32),
            pltpu.VMEM((TURNS, chunks, k, HALF), F32),
            pltpu.VMEM((chunks, k, HALF), F32),
            pltpu.VMEM((TURNS, chunks, k, HALF), F32),
            pltpu.VMEM((TURNS, chunks, 2, k, HALF), F32),
            pltpu.VMEM((k, wide), F32),
            pltpu.VMEM((ranks, lines, wide), F32),
            pltpu.VMEM((TURNS, ranks, lines, wide), F32),
            pltpu.VMEM((TURNS, lines, wide), F32),
            pltpu.VMEM((TURNS, ranks, lines, wide), F32),
            pltpu.VMEM((groups, k, k), F32),
            pltpu.VMEM((k, k), F32),
            pltpu.VMEM((ranks, k, k), F32),
            pltpu.VMEM((k, k), F32),
            pltpu.VMEM((k, k), F32),
            pltpu.VMEM((chunks, 2, k, HALF), F32),
            dma((SLOTS,)),
            dma,
            dma((TURNS, chunks)),
            dma((TURNS, chunks)),
            dma((TURNS, chunks)),
            dma((TURNS, chunks)),
            dma((TURNS, chunks)),
            dma((TURNS, chunks)),
            dma((TURNS, ranks)),
            dma((TURNS, ranks)),
            dma((TURNS, ranks)),
            dma((TURNS, ranks)),
            dma((groups,)),
            dma((groups,)),
            dma((ranks,)),
            dma((ranks,)),
        ],
        compiler_params=pltpu.CompilerParams(
            collective_id=0, has_side_effects=True, vmem_limit_bytes=58 * 1024 * 1024
        ),
        cost_estimate=pl.CostEstimate(
            flops=24 * rows_dev * width * k, bytes_accessed=rows_dev * width * 4, transcendentals=0
        ),
    )(stress, sketch)
    same = lambda i: (0, 0)
    return pl.pallas_call(
        functools.partial(finish, scale),
        grid=(per,),
        out_shape=(
            jax.ShapeDtypeStruct((k, share), F32),
            jax.ShapeDtypeStruct((k, width), F32),
            jax.ShapeDtypeStruct((k, k), F32),
        ),
        in_specs=[
            pl.BlockSpec((k, k), same),
            pl.BlockSpec((1, 2, k, HALF), lambda i: (i, 0, 0, 0)),
            pl.BlockSpec((k, width), same),
            pl.BlockSpec((k, k), same),
        ],
        out_specs=(
            pl.BlockSpec((k, CHUNK), lambda i: (0, i)),
            pl.BlockSpec((k, width), same),
            pl.BlockSpec((k, k), same),
        ),
    )(factor, part_out, coeffs, spectrum)


def solution(mesh):
    placed = (P("rows", "snaps"), P(None, "snaps"))
    return jax.shard_map(
        on_device,
        mesh=mesh,
        in_specs=placed,
        out_specs=(P(None, ("rows", "snaps")), P(None, "snaps"), P()),
        check_vma=False,
    )
```

profile of v0, /device:TPU:0, one launch (start us, length us, event | category | flops | bytes accessed | tf_op | source)
XLA Modules:
  0.0 147.4 jit_solution(1197516006856872138)
XLA Ops:
  0.6 142.7 %shard_map.49 = (f32[4,2,64,512]{3,2,1,0:T(8,128)}, f32[64,64]{1,0:T(8,128)}, f32[64,256]{1,0:T(8,128)}, f32[64,64]{1,0:T(8,128)}) custom-call(f32[16384,256]{1,0:T(8,128)} %stress.1, f32[64,256]{1,0:T(8,128)} %sketch.1), custom_call_target="tpu_custom_call" | custom-call | flops 6442450944 | bytes 16777216 | tf_op jit(solution)/shard_map/pallas_call | solution.py:310
  143.3 4.1 %shard_map.50 = (f32[64,4096]{1,0:T(8,128)}, f32[64,256]{1,0:T(8,128)}, f32[64,64]{1,0:T(8,128)}) custom-call(f32[64,64]{1,0:T(8,128)} %get-tuple-element.7.factor, f32[4,2,64,512]{3,2,1,0:T(8,128)} %get-tuple-element.8.share, f32[64,256]{1,0:T(8,128)} %get-tuple-element.9.coeffs, f32[64,64]{1,0:T(8,128)} %get-tuple-element.10.spectrum), custom_call_target="tpu_custom_call" | custom-call | tf_op jit(solution)/shard_map/pallas_call | solution.py:366
where the time goes:
time: 148 us; the launch traced here: 147 us
  Pallas kernels  147 us (99%)
    pallas_call x1, Pallas kernels, on_device(): pl.pallas_call(functools.partial(kernel, ranks, float(width * groups)), o...  143 us
    pallas_call x1, Pallas kernels, on_device(): pl.pallas_call(functools.partial(finish, scale), grid=(per,), out_shape=(...  4.09 us

commit v1 on v0

v1 whole, which is shorter than its diff:
```python
import functools
import math

import jax
import jax.numpy as jnp
from jax import lax
from jax.experimental import pallas as pl
from jax.experimental.pallas import tpu as pltpu
from jax.sharding import PartitionSpec as P

MESH = pl.DeviceIdType.MESH
F32 = jnp.float32
BF16 = jnp.bfloat16
CHUNK = 1024
HALF = CHUNK // 2
SLOTS = 4
PIECE = 128
PHASES = 4
LEAD = 5
EARLY = 3
LATE = 6


def dot(left_m, right_m, left_dim, right_dim, precision=None):
    return lax.dot_general(
        left_m,
        right_m,
        (((left_dim,), (right_dim,)), ((), ())),
        precision=precision,
        preferred_element_type=F32,
    )


def dot_full(left_m, right_m, left_dim, right_dim):
    return dot(left_m, right_m, left_dim, right_dim, lax.Precision.HIGHEST)


def split(value):
    high = value.astype(BF16)
    low = (value - high.astype(F32)).astype(BF16)
    return high, low


def inverse_factor(gram):
    k = gram.shape[0]
    line = lax.broadcasted_iota(jnp.int32, (k, k), 0)
    lane = lax.broadcasted_iota(jnp.int32, (k, k), 1)
    wide_line = lax.broadcasted_iota(jnp.int32, (k, 2 * k), 0)
    ident = jnp.where(line == lane, 1.0, 0.0).astype(F32)
    table = jnp.concatenate([gram, ident], axis=1)
    for j in range(k - 1):
        row = table[j : j + 1, :]
        row = row / row[:, j : j + 1]
        column = jnp.where(wide_line > j, table[:, j : j + 1], 0.0)
        table = table - column * row
    diag = jnp.sum(jnp.where(line == lane, table[:, :k], 0.0), axis=1, keepdims=True)
    return table[:, k:] / jnp.sqrt(diag)


def solve_first(zone, width):
    h = zone.shape[0]
    f11 = inverse_factor(zone[:, width : width + h])
    return f11, dot_full(f11, zone[:, 0:width], 1, 0)


def solve_second(gram, f11):
    h = f11.shape[0]
    l21 = dot_full(gram[:, 0:h], f11, 1, 1)
    f22 = inverse_factor(gram[:, h : 2 * h] - dot_full(l21, l21, 1, 1))
    f21 = -dot_full(f22, dot_full(l21, f11, 1, 0), 1, 0)
    return f21, f22


def kernel(
    ranks, batch_total,
    stress, sketch, share_out, factor_out, coeffs_out, spectrum_out,
    stage, high, low, operand, later, part, got1, summed, got2, panel,
    acc, spread, landed, total, full, zone, first, spect, gram, grams, lead_factor,
    stage_sem, share_sem, send1, recv1, send2, recv2, send3, recv3,
    rs_send, rs_recv, ag_send, ag_recv, sp_send, sp_recv, gr_send, gr_recv,
):
    groups = 4
    k = sketch.shape[0]
    kp = k // 2
    width = stress.shape[1]
    chunks = summed.shape[0]
    lines = kp // ranks
    me_row = lax.axis_index("rows")
    me = lax.axis_index("snaps")
    mine = me % 2
    core = me + 1 - 2 * mine
    chip = (me + 2) % groups
    units = PHASES * chunks

    def load(c):
        slot = c % SLOTS
        return pltpu.make_async_copy(
            stress.at[pl.ds(c * CHUNK, CHUNK), :], stage.at[slot], stage_sem.at[slot]
        )

    for c in range(SLOTS):
        load(c).start()

    barrier = pltpu.get_barrier_semaphore()
    for d in range(1, ranks):
        pl.semaphore_signal(
            barrier, inc=1, device_id={"rows": (me_row + d) % ranks}, device_id_type=MESH
        )
    for d in range(1, groups):
        pl.semaphore_signal(
            barrier, inc=1, device_id={"snaps": (me + d) % groups}, device_id_type=MESH
        )

    def remote(src, dst, s_sem, r_sem, device):
        return pltpu.make_async_remote_copy(
            src_ref=src, dst_ref=dst, send_sem=s_sem, recv_sem=r_sem,
            device_id=device, device_id_type=MESH,
        )

    def hop1(p, c):
        return remote(
            part.at[p % 2, c, 1 - mine], got1.at[p, c], send1.at[p, c], recv1.at[p, c],
            {"snaps": core},
        )

    def hop2(p, c):
        return remote(summed.at[c], got2.at[p, c], send2.at[p, c], recv2.at[p, c], {"snaps": chip})

    def hop3(p, c):
        return remote(
            panel.at[p, c, mine], panel.at[p, c, mine], send3.at[p, c], recv3.at[p, c],
            {"snaps": core},
        )

    def scatter(p, d):
        to = (me_row + d) % ranks
        return remote(
            spread.at[p, to], landed.at[p, d], rs_send.at[p, d], rs_recv.at[p, d], {"rows": to}
        )

    def gather(p, d):
        to = (me_row + d) % ranks
        return remote(
            total.at[p], full.at[p, me_row], ag_send.at[p, d], ag_recv.at[p, d], {"rows": to}
        )

    def give_gram(d):
        return remote(
            gram, grams.at[me_row], gr_send.at[d], gr_recv.at[d], {"rows": (me_row + d) % ranks}
        )

    def share_spectrum(d):
        return remote(
            spect.at[0], spect.at[d], sp_send.at[d], sp_recv.at[d], {"snaps": (me + d) % groups}
        )

    def share_copy(i):
        per = chunks // groups
        return pltpu.make_async_copy(
            panel.at[2 + i, pl.ds(me * per, per)],
            share_out.at[i],
            share_sem.at[i],
        )

    def convert(c):
        slot = c % SLOTS
        load(c).wait()

        def body(p, carry):
            h, l = split(stage[slot, pl.ds(p * PIECE, PIECE), :])
            at = pl.ds(c * CHUNK + p * PIECE, PIECE)
            high[at, :] = h
            low[at, :] = l
            return carry

        lax.fori_loop(0, CHUNK // PIECE, body, 0)

        @pl.when(c + SLOTS < chunks)
        def _():
            load(c + SLOTS).start()

    def produce(p, c):
        @pl.when(p == 0)
        def _():
            convert(c)
            for h in range(2):
                at = pl.ds(c * CHUNK + h * HALF, HALF)
                both = dot(operand[...], high[at, :], 1, 1)
                rest = dot(operand[0:k, :], low[at, :], 1, 1)
                value = both[0:k] + (both[k : 2 * k] + rest)
                part[0, c, h] = value[0:kp]
                part[1, c, h] = value[kp:k]

        @pl.when(p >= 2)
        def _():
            i = p % 2
            for h in range(2):
                at = pl.ds(c * CHUNK + h * HALF, HALF)
                both = dot(later[i], high[at, :], 1, 1)
                rest = dot(later[i, 0:kp, :], low[at, :], 1, 1)
                part[i, c, h] = both[0:kp] + (both[kp:k] + rest)

        hop1(p, c).start()

    def add_cores(p, c):
        hop1(p, c).wait()
        summed[c] = part[p % 2, c, mine] + got1[p, c]
        hop2(p, c).start()

    def add_chips(p, c):
        hop2(p, c).wait()
        panel[p, c, mine] = summed[c] + got2[p, c]
        hop3(p, c).start()

    def accumulate(p, c):
        hop3(p, c).wait()
        for h in range(2):
            value = panel[p, c, h]
            hi, lo = split(value)
            at = pl.ds(c * CHUNK + h * HALF, HALF)
            both = dot(jnp.concatenate([hi, lo], axis=0), high[at, :], 1, 0)
            rest = dot(hi, low[at, :], 1, 0)
            acc[:, 0:width] += both[0:kp] + (both[kp:k] + rest)

        @pl.when(p % 2 == 0)
        def _():
            for h in range(2):
                value = panel[p, c, h]
                acc[:, width : width + kp] += dot_full(value, value, 1, 1)

        @pl.when(p % 2 == 1)
        def _():
            for h in range(2):
                value = panel[p, c, h]
                pair = jnp.concatenate([panel[p - 1, c, h], value], axis=0)
                acc[:, width : width + k] += dot_full(value, pair, 1, 1)

    def reduce_start(p):
        for r in range(ranks):
            spread[p, r] = acc[r * lines : (r + 1) * lines, :]
        acc[...] = jnp.zeros_like(acc)
        for d in range(1, ranks):
            scatter(p, d).start()

    def reduce_share(p):
        value = spread[p, me_row]
        for d in range(1, ranks):
            scatter(p, d).wait()
            value = value + landed[p, d]
        total[p] = value
        full[p, me_row] = value
        for d in range(1, ranks):
            gather(p, d).start()

    def reduce_end(p):
        for d in range(1, ranks):
            gather(p, d).wait()
        for r in range(ranks):
            zone[r * lines : (r + 1) * lines, :] = full[p, r]

    def set_later(i, value):
        h, l = split(value)
        later[i, 0:kp, :] = h
        later[i, kp:k, :] = l

    h, l = split(sketch[...])
    operand[0:k, :] = h
    operand[k : 2 * k, :] = l
    acc[...] = jnp.zeros_like(acc)
    pl.semaphore_wait(barrier, ranks - 1 + groups - 1)
    wait1, wait2 = EARLY * chunks // 16, LATE * chunks // 16

    def step(s, carry):
        @pl.when(s < units)
        def _():
            produce(s // chunks, s % chunks)

        @pl.when(jnp.logical_and(s >= 1, s <= units))
        def _():
            u = s - 1
            add_cores(u // chunks, u % chunks)

        @pl.when(jnp.logical_and(s >= 1 + LEAD, s <= units + LEAD))
        def _():
            u = s - 1 - LEAD
            add_chips(u // chunks, u % chunks)

        @pl.when(s >= 2 + LEAD)
        def _():
            u = s - 2 - LEAD
            accumulate(u // chunks, u % chunks)

        since = s - (chunks + LEAD + 1)
        done = since // chunks
        at = since % chunks
        live = jnp.logical_and(since >= 0, done < PHASES - 1)

        @pl.when(jnp.logical_and(live, at == 0))
        def _():
            reduce_start(done)

        @pl.when(jnp.logical_and(live, at == wait1))
        def _():
            reduce_share(done)

        @pl.when(jnp.logical_and(live, at == wait2))
        def _():
            reduce_end(done)

            @pl.when(done % 2 == 0)
            def _():
                f11, value = solve_first(zone[...], width)
                lead_factor[...] = f11
                first[0] = zone[:, 0:width]
                first[1] = value
                set_later(0, value)

            @pl.when(done % 2 == 1)
            def _():
                f21, f22 = solve_second(zone[:, width : width + k], lead_factor[...])
                value = dot_full(f21, first[0], 1, 0) + dot_full(f22, zone[:, 0:width], 1, 0)
                set_later(1, value)

        return carry

    lax.fori_loop(0, units + LEAD + 2, step, 0)

    own_gram = acc[:, width : width + k]
    gram[...] = own_gram
    grams[me_row] = own_gram
    for d in range(1, ranks):
        give_gram(d).start()
    reduce_start(3)
    for i in range(2):
        share_copy(i).start()
    for d in range(1, ranks):
        give_gram(d).wait_recv()
    gram_total = grams[0]
    for r in range(1, ranks):
        gram_total = gram_total + grams[r]
    reduce_share(3)
    f21, f22 = solve_second(gram_total, lead_factor[...])
    factor_out[0:kp, :] = jnp.concatenate([lead_factor[...], jnp.zeros((kp, kp), F32)], axis=1)
    factor_out[kp:k, :] = jnp.concatenate([f21, f22], axis=1)
    reduce_end(3)
    coeffs_out[0:kp, :] = first[1]
    coeffs_out[kp:k, :] = dot_full(f21, first[0], 1, 0) + dot_full(f22, zone[:, 0:width], 1, 0)
    sums = coeffs_out[...]
    spect[0] = dot_full(sums, sums, 1, 1)
    for d in range(1, groups):
        share_spectrum(d).start()
    for d in range(1, ranks):
        give_gram(d).wait_send()
    for i in range(2):
        share_copy(i).wait()
    for d in range(1, groups):
        share_spectrum(d).wait()
    a = spect[0] + spect[2]
    b = spect[1] + spect[3]
    spectrum_out[...] = (a + b) / batch_total


def finish(scale, factor, share, coeffs, spectrum, basis_out, coeffs_out, spectrum_out):
    scaled = factor[...] * scale
    for h in range(2):
        both = jnp.concatenate([share[0, 0, h], share[1, 0, h]], axis=0)
        basis_out[:, h * HALF : (h + 1) * HALF] = dot_full(scaled, both, 1, 0)
    coeffs_out[...] = coeffs[...]
    spectrum_out[...] = spectrum[...]


def on_device(stress, sketch):
    rows_dev, width = stress.shape
    k = sketch.shape[0]
    kp = k // 2
    groups = lax.axis_size("snaps")
    ranks = lax.axis_size("rows")
    share = rows_dev // groups
    chunks = rows_dev // CHUNK
    lines = kp // ranks
    wide = width + 128
    scale = math.sqrt(float(rows_dev * ranks))
    vmem = pl.BlockSpec(memory_space=pltpu.VMEM)
    dma = pltpu.SemaphoreType.DMA
    per = chunks // groups
    part_out, factor, coeffs, spectrum = pl.pallas_call(
        functools.partial(kernel, ranks, float(width * groups)),
        out_shape=(
            jax.ShapeDtypeStruct((2, per, 2, kp, HALF), F32),
            jax.ShapeDtypeStruct((k, k), F32),
            jax.ShapeDtypeStruct((k, width), F32),
            jax.ShapeDtypeStruct((k, k), F32),
        ),
        in_specs=[pl.BlockSpec(memory_space=pl.ANY), vmem],
        out_specs=(pl.BlockSpec(memory_space=pl.ANY), vmem, vmem, vmem),
        scratch_shapes=[
            pltpu.VMEM((SLOTS, CHUNK, width), F32),
            pltpu.VMEM((rows_dev, width), BF16),
            pltpu.VMEM((rows_dev, width), BF16),
            pltpu.VMEM((2 * k, width), BF16),
            pltpu.VMEM((2, k, width), BF16),
            pltpu.VMEM((2, chunks, 2, kp, HALF), F32),
            pltpu.VMEM((PHASES, chunks, kp, HALF), F32),
            pltpu.VMEM((chunks, kp, HALF), F32),
            pltpu.VMEM((PHASES, chunks, kp, HALF), F32),
            pltpu.VMEM((PHASES, chunks, 2, kp, HALF), F32),
            pltpu.VMEM((kp, wide), F32),
            pltpu.VMEM((PHASES, ranks, lines, wide), F32),
            pltpu.VMEM((PHASES, ranks, lines, wide), F32),
            pltpu.VMEM((PHASES, lines, wide), F32),
            pltpu.VMEM((PHASES, ranks, lines, wide), F32),
            pltpu.VMEM((kp, wide), F32),
            pltpu.VMEM((2, kp, width), F32),
            pltpu.VMEM((groups, k, k), F32),
            pltpu.VMEM((kp, k), F32),
            pltpu.VMEM((ranks, kp, k), F32),
            pltpu.VMEM((kp, kp), F32),
            dma((SLOTS,)),
            dma((2,)),
            dma((PHASES, chunks)),
            dma((PHASES, chunks)),
            dma((PHASES, chunks)),
            dma((PHASES, chunks)),
            dma((PHASES, chunks)),
            dma((PHASES, chunks)),
            dma((PHASES, ranks)),
            dma((PHASES, ranks)),
            dma((PHASES, ranks)),
            dma((PHASES, ranks)),
            dma((groups,)),
            dma((groups,)),
            dma((ranks,)),
            dma((ranks,)),
        ],
        compiler_params=pltpu.CompilerParams(
            collective_id=0, has_side_effects=True, vmem_limit_bytes=58 * 1024 * 1024
        ),
        cost_estimate=pl.CostEstimate(
            flops=24 * rows_dev * width * k, bytes_accessed=rows_dev * width * 4, transcendentals=0
        ),
    )(stress, sketch)
    same = lambda i: (0, 0)
    return pl.pallas_call(
        functools.partial(finish, scale),
        grid=(per,),
        out_shape=(
            jax.ShapeDtypeStruct((k, share), F32),
            jax.ShapeDtypeStruct((k, width), F32),
            jax.ShapeDtypeStruct((k, k), F32),
        ),
        in_specs=[
            pl.BlockSpec((k, k), same),
            pl.BlockSpec((2, 1, 2, kp, HALF), lambda i: (0, i, 0, 0, 0)),
            pl.BlockSpec((k, width), same),
            pl.BlockSpec((k, k), same),
        ],
        out_specs=(
            pl.BlockSpec((k, CHUNK), lambda i: (0, i)),
            pl.BlockSpec((k, width), same),
            pl.BlockSpec((k, k), same),
        ),
    )(factor, part_out, coeffs, spectrum)


def solution(mesh):
    placed = (P("rows", "snaps"), P(None, "snaps"))
    return jax.shard_map(
        on_device,
        mesh=mesh,
        in_specs=placed,
        out_specs=(P(None, ("rows", "snaps")), P(None, "snaps"), P()),
        check_vma=False,
    )
```

time: 148 us -> 127 us (0.86)
  Pallas kernels: 147 us -> 126 us
    pallas_call x1, Pallas kernels: 143 us -> 122 us  [on_device(): pl.pallas_call(functools.partial(kernel, ranks, float(width * groups)), o...]
where the time goes in v1:
time: 127 us; the launch traced here: 126 us
  Pallas kernels  126 us (99%)
    pallas_call x1, Pallas kernels, on_device(): pl.pallas_call(functools.partial(kernel, ranks, float(width * groups)), o...  122 us
    pallas_call x1, Pallas kernels, on_device(): pl.pallas_call(functools.partial(finish, scale), grid=(per,), out_shape=(...  4.09 us

profile of v1, /device:TPU:0, one launch (start us, length us, event | category | flops | bytes accessed | tf_op | source)
XLA Modules:
  0.0 126.3 jit_solution(11203522664436801990)
XLA Ops:
  0.6 121.6 %shard_map.49 = (f32[2,4,2,32,512]{4,3,2,1,0:T(8,128)}, f32[64,64]{1,0:T(8,128)}, f32[64,256]{1,0:T(8,128)}, f32[64,64]{1,0:T(8,128)}) custom-call(f32[16384,256]{1,0:T(8,128)} %stress.1, f32[64,256]{1,0:T(8,128)} %sketch.1), custom_call_target="tpu_custom_call" | custom-call | flops 6442450944 | bytes 16777216 | tf_op jit(solution)/shard_map/pallas_call | solution.py:386
  122.2 4.1 %shard_map.50 = (f32[64,4096]{1,0:T(8,128)}, f32[64,256]{1,0:T(8,128)}, f32[64,64]{1,0:T(8,128)}) custom-call(f32[64,64]{1,0:T(8,128)} %get-tuple-element.7.factor, f32[2,4,2,32,512]{4,3,2,1,0:T(8,128)} %get-tuple-element.8.share, f32[64,256]{1,0:T(8,128)} %get-tuple-element.9.coeffs, f32[64,64]{1,0:T(8,128)} %get-tuple-element.10.spectrum), custom_call_target="tpu_custom_call" | custom-call | tf_op jit(solution)/shard_map/pallas_call | solution.py:443

commit v2 on v1

v2 whole, which is shorter than its diff:
```python
import functools
import math

import jax
import jax.numpy as jnp
from jax import lax
from jax.experimental import pallas as pl
from jax.experimental.pallas import tpu as pltpu
from jax.sharding import PartitionSpec as P

MESH = pl.DeviceIdType.MESH
F32 = jnp.float32
BF16 = jnp.bfloat16
CHUNK = 2048
HALF = CHUNK // 2
SLOTS = 2
PIECE = 128
CUTS = 4
PIECES = 4
PHASES = 4
LEAD = 3
EARLY = 3
LATE = 6
PAIR = 1
BACK = 1


def dot(left_m, right_m, left_dim, right_dim, precision=None):
    return lax.dot_general(
        left_m,
        right_m,
        (((left_dim,), (right_dim,)), ((), ())),
        precision=precision,
        preferred_element_type=F32,
    )


def dot_full(left_m, right_m, left_dim, right_dim):
    return dot(left_m, right_m, left_dim, right_dim, lax.Precision.HIGHEST)


def split(value):
    high = value.astype(BF16)
    low = (value - high.astype(F32)).astype(BF16)
    return high, low


def inverse_factor(gram):
    k = gram.shape[0]
    line = lax.broadcasted_iota(jnp.int32, (k, k), 0)
    lane = lax.broadcasted_iota(jnp.int32, (k, k), 1)
    wide_line = lax.broadcasted_iota(jnp.int32, (k, 2 * k), 0)
    ident = jnp.where(line == lane, 1.0, 0.0).astype(F32)
    table = jnp.concatenate([gram, ident], axis=1)
    for j in range(k - 1):
        row = table[j : j + 1, :]
        row = row / row[:, j : j + 1]
        column = jnp.where(wide_line > j, table[:, j : j + 1], 0.0)
        table = table - column * row
    diag = jnp.sum(jnp.where(line == lane, table[:, :k], 0.0), axis=1, keepdims=True)
    return table[:, k:] / jnp.sqrt(diag)


def below(gram, f11):
    h = f11.shape[0]
    l21 = dot_full(gram[:, 0:h], f11, 1, 1)
    return l21, gram[:, h : 2 * h] - dot_full(l21, l21, 1, 1)


def kernel(
    ranks, batch_total, scale,
    stress, sketch, basis_out, coeffs_out, spectrum_out,
    stage, high, low, operand, part, got1, summed, got2, panel,
    acc, gacc, spread, landed, total, full, zone, lead, basis, spect, gram, grams, lead_factor,
    stage_sem, basis_sem, send1, recv1, send2, recv2, send3, recv3,
    rs_send, rs_recv, ag_send, ag_recv, sp_send, sp_recv, gr_send, gr_recv,
):
    groups = 4
    k = sketch.shape[0]
    kp = k // 2
    width = stress.shape[1]
    chunks = summed.shape[0]
    lines = kp // ranks
    me_row = lax.axis_index("rows")
    me = lax.axis_index("snaps")
    mine = me % 2
    core = me + 1 - 2 * mine
    chip = (me + 2) % groups
    units = PHASES * chunks
    per = chunks // groups
    blocks = [(i, h, (2 * i + h) * HALF) for i in range(per) for h in range(2)]

    def load(c, q):
        slot = c % SLOTS
        rows = CHUNK // CUTS
        return pltpu.make_async_copy(
            stress.at[pl.ds(c * CHUNK + q * rows, rows), :],
            stage.at[slot, pl.ds(q * rows, rows), :],
            stage_sem.at[slot, q],
        )

    for q in range(CUTS):
        load(0, q).start()

    barrier = pltpu.get_barrier_semaphore()
    for d in range(1, ranks):
        pl.semaphore_signal(
            barrier, inc=1, device_id={"rows": (me_row + d) % ranks}, device_id_type=MESH
        )
    for d in range(1, groups):
        pl.semaphore_signal(
            barrier, inc=1, device_id={"snaps": (me + d) % groups}, device_id_type=MESH
        )

    def remote(src, dst, s_sem, r_sem, device):
        return pltpu.make_async_remote_copy(
            src_ref=src, dst_ref=dst, send_sem=s_sem, recv_sem=r_sem,
            device_id=device, device_id_type=MESH,
        )

    def hop1(p, c):
        return remote(
            part.at[c, 1 - mine], got1.at[p, c], send1.at[p, c], recv1.at[p, c],
            {"snaps": core},
        )

    def hop2(p, c):
        return remote(summed.at[c], got2.at[p, c], send2.at[p, c], recv2.at[p, c], {"snaps": chip})

    def hop3(p, c):
        return remote(
            panel.at[p, c, mine], panel.at[p, c, mine], send3.at[p, c], recv3.at[p, c],
            {"snaps": core},
        )

    def scatter(p, d, lanes=None):
        to = (me_row + d) % ranks
        src, dst = spread.at[p, to], landed.at[p, d]
        if lanes is not None:
            src, dst = src.at[:, 0:lanes], dst.at[:, 0:lanes]
        return remote(src, dst, rs_send.at[p, d], rs_recv.at[p, d], {"rows": to})

    def gather(p, d, lanes=None):
        to = (me_row + d) % ranks
        src, dst = total.at[p], full.at[p, me_row]
        if lanes is not None:
            src, dst = src.at[:, 0:lanes], dst.at[:, 0:lanes]
        return remote(src, dst, ag_send.at[p, d], ag_recv.at[p, d], {"rows": to})

    def give_gram(d):
        return remote(
            gram, grams.at[me_row], gr_send.at[d], gr_recv.at[d], {"rows": (me_row + d) % ranks}
        )

    def share_spectrum(d):
        return remote(
            spect.at[0], spect.at[d], sp_send.at[d], sp_recv.at[d], {"snaps": (me + d) % groups}
        )

    def basis_copy(i):
        at = pl.ds(i * kp, kp)
        return pltpu.make_async_copy(basis.at[at, :], basis_out.at[at, :], basis_sem.at[i])

    def convert(c):
        slot = c % SLOTS

        @pl.when(c + 1 < chunks)
        def _():
            for q in range(CUTS):
                load(c + 1, q).start()

        per_cut = CHUNK // CUTS // PIECE
        for q in range(CUTS):
            load(c, q).wait()

            def body(i, carry):
                h, l = split(stage[slot, pl.ds(i * PIECE, PIECE), :])
                at = pl.ds(c * CHUNK + i * PIECE, PIECE)
                high[at, :] = h
                low[at, :] = l
                return carry

            lax.fori_loop(q * per_cut, (q + 1) * per_cut, body, 0)

    def project(p, c, h):
        at = pl.ds(c * CHUNK + h * HALF, HALF)
        both = dot(operand[p], high[at, :], 1, 1)
        rest = dot(operand[p, 0:kp, :], low[at, :], 1, 1)
        part[c, h] = both[0:kp] + (both[kp:k] + rest)

    def produce(p, c):
        @pl.when(p == 0)
        def _():
            convert(c)

        project(p, c, 1 - mine)

        @pl.when(jnp.logical_and(p == 0, c == 0))
        def _():
            pl.semaphore_wait(barrier, ranks - 1 + groups - 1)

        hop1(p, c).start()
        project(p, c, mine)

    def add_cores(p, c):
        hop1(p, c).wait()
        summed[c] = part[c, mine] + got1[p, c]
        hop2(p, c).start()

    def add_chips(p, c):
        hop2(p, c).wait()
        panel[p, c, mine] = summed[c] + got2[p, c]
        hop3(p, c).start()

    def stacked(p, c):
        value = jnp.concatenate([panel[p, c, 0], panel[p, c, 1]], axis=1)
        hi, lo = split(value)
        return jnp.concatenate([hi, lo], axis=0)

    def accumulate(p, c):
        hop3(p, c).wait()
        stack = stacked(p, c)
        at = pl.ds(c * CHUNK, CHUNK)
        both = dot(stack, high[at, :], 1, 0)
        rest = dot(stack[0:kp], low[at, :], 1, 0)
        acc[:, 0:width] += both[0:kp] + (both[kp:k] + rest)

        @pl.when(p % 2 == 0)
        def _():
            gacc[:, 0:k] += dot(stack, stack, 1, 1)

        @pl.when(p % 2 == 1)
        def _():
            gacc[...] += dot(stack, jnp.concatenate([stacked(p - 1, c), stack], axis=0), 1, 1)

    def fold_gram():
        rows = gacc[0:kp, :] + gacc[kp:k, :]
        for i in range(2):
            at = i * k
            acc[:, width + i * kp : width + (i + 1) * kp] = (
                rows[:, at : at + kp] + rows[:, at + kp : at + k]
            )
        gacc[...] = jnp.zeros_like(gacc)

    def reduce_start(p, lanes=None):
        for r in range(ranks):
            spread[p, r] = acc[r * lines : (r + 1) * lines, :]
        acc[...] = jnp.zeros_like(acc)
        for d in range(1, ranks):
            scatter(p, d, lanes).start()

    def reduce_share(p, lanes=None):
        value = spread[p, me_row]
        for d in range(1, ranks):
            scatter(p, d, lanes).wait()
            value = value + landed[p, d]
        total[p] = value
        full[p, me_row] = value
        for d in range(1, ranks):
            gather(p, d, lanes).start()

    def reduce_end(p, lanes=None):
        for d in range(1, ranks):
            gather(p, d, lanes).wait()
        for r in range(ranks):
            zone[r * lines : (r + 1) * lines, :] = full[p, r]

    def set_operand(p, value):
        h, l = split(value)
        operand[p, 0:kp, :] = h
        operand[p, kp:k, :] = l

    for i in range(2):
        set_operand(i, sketch[i * kp : (i + 1) * kp, :])
    acc[...] = jnp.zeros_like(acc)
    gacc[...] = jnp.zeros_like(gacc)
    wait1, wait2 = EARLY * chunks // 16, LATE * chunks // 16

    def step(s, carry):
        @pl.when(s < units)
        def _():
            produce(s // chunks, s % chunks)

        @pl.when(jnp.logical_and(s >= PAIR, s < units + PAIR))
        def _():
            u = s - PAIR
            add_cores(u // chunks, u % chunks)

        @pl.when(jnp.logical_and(s >= PAIR + LEAD, s < units + PAIR + LEAD))
        def _():
            u = s - PAIR - LEAD
            add_chips(u // chunks, u % chunks)

        @pl.when(s >= PAIR + LEAD + BACK)
        def _():
            u = s - PAIR - LEAD - BACK
            accumulate(u // chunks, u % chunks)

        since = s - (chunks - 1 + PAIR + LEAD + BACK)
        done = since // chunks
        at = since % chunks
        live = jnp.logical_and(since >= 0, done < PHASES - 1)

        @pl.when(jnp.logical_and(live, at == 0))
        def _():
            fold_gram()
            reduce_start(done)

        @pl.when(jnp.logical_and(live, at == wait1))
        def _():
            reduce_share(done)

        @pl.when(jnp.logical_and(live, at == wait2))
        def _():
            reduce_end(done)

            @pl.when(done % 2 == 0)
            def _():
                f11 = inverse_factor(zone[:, width : width + kp])
                value = dot_full(f11, zone[:, 0:width], 1, 0)
                lead_factor[...] = f11
                lead[...] = value
                set_operand(2, value)

            @pl.when(done == 1)
            def _():
                l21, rest = below(zone[:, width : width + k], lead_factor[...])
                f22 = inverse_factor(rest)
                value = zone[:, 0:width] - dot_full(l21, lead[...], 1, 0)
                set_operand(3, dot_full(f22, value, 1, 0))

            @pl.when(done == 2)
            def _():
                scaled = lead_factor[...] * scale
                for i, h, at in blocks:
                    value = panel[2, me * per + i, h]
                    basis[0:kp, at : at + HALF] = dot_full(scaled, value, 1, 0)
                basis_copy(0).start()

        return carry

    lax.fori_loop(0, units + PAIR + LEAD + BACK, step, 0)

    fold_gram()
    own_gram = acc[:, width : width + k]
    gram[...] = own_gram
    grams[me_row] = own_gram
    reduce_start(3, width)
    for d in range(1, ranks):
        give_gram(d).start()
    reduce_share(3, width)
    for d in range(1, ranks):
        give_gram(d).wait_recv()
    gram_total = grams[0]
    for r in range(1, ranks):
        gram_total = gram_total + grams[r]
    l21, rest = below(gram_total, lead_factor[...])
    top = lead[...]
    f22 = inverse_factor(rest)
    low_top = dot_full(l21, top, 1, 0)
    for i, h, at in blocks:
        value = panel[3, me * per + i, h]
        basis[kp:k, at : at + HALF] = scale * value - dot_full(l21, basis[0:kp, at : at + HALF], 1, 0)
    reduce_end(3, width)
    sums = jnp.concatenate([top, dot_full(f22, zone[:, 0:width] - low_top, 1, 0)], axis=0)
    coeffs_out[...] = sums
    spect[0] = dot_full(sums, sums, 1, 1)
    for d in range(1, groups):
        share_spectrum(d).start()
    for i, h, at in blocks:
        basis[kp:k, at : at + HALF] = dot_full(f22, basis[kp:k, at : at + HALF], 1, 0)
    basis_copy(1).start()
    for d in range(1, ranks):
        give_gram(d).wait_send()
    for d in range(1, groups):
        share_spectrum(d).wait()
    a = spect[0] + spect[2]
    b = spect[1] + spect[3]
    spectrum_out[...] = (a + b) / batch_total
    for i in range(2):
        basis_copy(i).wait()


def finish(basis, coeffs, spectrum, basis_out, coeffs_out, spectrum_out, hold, rows, tiny, came, went):
    lines = basis.shape[0] // PIECES
    routes = [(coeffs, rows, coeffs_out), (spectrum, tiny, spectrum_out)]
    for i in range(PIECES):
        at = pl.ds(i * lines, lines)
        routes.append((basis.at[at, :], hold.at[at, :], basis_out.at[at, :]))
    loads = [pltpu.make_async_copy(r[0], r[1], came.at[i]) for i, r in enumerate(routes)]
    stores = [pltpu.make_async_copy(r[1], r[2], went.at[i]) for i, r in enumerate(routes)]
    for load in loads:
        load.start()
    for load, store in zip(loads, stores):
        load.wait()
        store.start()
    for store in stores:
        store.wait()


def on_device(stress, sketch):
    rows_dev, width = stress.shape
    k = sketch.shape[0]
    kp = k // 2
    groups = lax.axis_size("snaps")
    ranks = lax.axis_size("rows")
    share = rows_dev // groups
    chunks = rows_dev // CHUNK
    lines = kp // ranks
    wide = width + 128
    scale = math.sqrt(float(rows_dev * ranks))
    vmem = pl.BlockSpec(memory_space=pltpu.VMEM)
    dma = pltpu.SemaphoreType.DMA
    found = pl.pallas_call(
        functools.partial(kernel, ranks, float(width * groups), scale),
        out_shape=(
            jax.ShapeDtypeStruct((k, share), F32),
            jax.ShapeDtypeStruct((k, width), F32),
            jax.ShapeDtypeStruct((k, k), F32),
        ),
        in_specs=[pl.BlockSpec(memory_space=pl.ANY), vmem],
        out_specs=(pl.BlockSpec(memory_space=pl.ANY), vmem, vmem),
        scratch_shapes=[
            pltpu.VMEM((SLOTS, CHUNK, width), F32),
            pltpu.VMEM((rows_dev, width), BF16),
            pltpu.VMEM((rows_dev, width), BF16),
            pltpu.VMEM((PHASES, k, width), BF16),
            pltpu.VMEM((chunks, 2, kp, HALF), F32),
            pltpu.VMEM((PHASES, chunks, kp, HALF), F32),
            pltpu.VMEM((chunks, kp, HALF), F32),
            pltpu.VMEM((PHASES, chunks, kp, HALF), F32),
            pltpu.VMEM((PHASES, chunks, 2, kp, HALF), F32),
            pltpu.VMEM((kp, wide), F32),
            pltpu.VMEM((k, 2 * k), F32),
            pltpu.VMEM((PHASES, ranks, lines, wide), F32),
            pltpu.VMEM((PHASES, ranks, lines, wide), F32),
            pltpu.VMEM((PHASES, lines, wide), F32),
            pltpu.VMEM((PHASES, ranks, lines, wide), F32),
            pltpu.VMEM((kp, wide), F32),
            pltpu.VMEM((kp, width), F32),
            pltpu.VMEM((k, share), F32),
            pltpu.VMEM((groups, k, k), F32),
            pltpu.VMEM((kp, k), F32),
            pltpu.VMEM((ranks, kp, k), F32),
            pltpu.VMEM((kp, kp), F32),
            dma((SLOTS, CUTS)),
            dma((2,)),
            dma((PHASES, chunks)),
            dma((PHASES, chunks)),
            dma((PHASES, chunks)),
            dma((PHASES, chunks)),
            dma((PHASES, chunks)),
            dma((PHASES, chunks)),
            dma((PHASES, ranks)),
            dma((PHASES, ranks)),
            dma((PHASES, ranks)),
            dma((PHASES, ranks)),
            dma((groups,)),
            dma((groups,)),
            dma((ranks,)),
            dma((ranks,)),
        ],
        compiler_params=pltpu.CompilerParams(
            collective_id=0, has_side_effects=True, vmem_limit_bytes=58 * 1024 * 1024
        ),
        cost_estimate=pl.CostEstimate(
            flops=24 * rows_dev * width * k, bytes_accessed=rows_dev * width * 4, transcendentals=0
        ),
    )(stress, sketch)
    anywhere = pl.BlockSpec(memory_space=pl.ANY)
    return pl.pallas_call(
        finish,
        out_shape=tuple(jax.ShapeDtypeStruct(a.shape, a.dtype) for a in found),
        in_specs=[anywhere] * 3,
        out_specs=(anywhere,) * 3,
        scratch_shapes=[
            pltpu.VMEM((k, share), F32),
            pltpu.VMEM((k, width), F32),
            pltpu.VMEM((k, k), F32),
            dma((PIECES + 2,)),
            dma((PIECES + 2,)),
        ],
    )(*found)


def solution(mesh):
    placed = (P("rows", "snaps"), P(None, "snaps"))
    return jax.shard_map(
        on_device,
        mesh=mesh,
        in_specs=placed,
        out_specs=(P(None, ("rows", "snaps")), P(None, "snaps"), P()),
        check_vma=False,
    )
```

time: 127 us -> 120 us (0.945)
  Pallas kernels: 126 us -> 120 us
    pallas_call x2, Pallas kernels: 126 us -> 120 us  [the longest x1 117 us: on_device(): pl.pallas_call(functools.partial(kernel, ranks, float(width * groups), sc...]
where the time goes in v2:
time: 120 us
  Pallas kernels  120 us (100%)
    pallas_call x1, Pallas kernels, on_device(): pl.pallas_call(functools.partial(kernel, ranks, float(width * groups), sc...  117 us

profile of v2, /device:TPU:0, one launch (start us, length us, event | category | flops | bytes accessed | tf_op | source)
XLA Modules:
  0.0 120.2 jit_solution(2612259546082413190)
XLA Ops:
  0.6 117.5 %shard_map.49 = (f32[64,4096]{1,0:T(8,128)}, f32[64,256]{1,0:T(8,128)}, f32[64,64]{1,0:T(8,128)}) custom-call(f32[16384,256]{1,0:T(8,128)} %stress.1, f32[64,256]{1,0:T(8,128)} %sketch.1), custom_call_target="tpu_custom_call" | custom-call | flops 6442450944 | bytes 16777216 | tf_op jit(solution)/shard_map/pallas_call | solution.py:414
  118.1 2.1 %shard_map.50 = (f32[64,4096]{1,0:T(8,128)}, f32[64,256]{1,0:T(8,128)}, f32[64,64]{1,0:T(8,128)}) custom-call(f32[64,4096]{1,0:T(8,128)} %get-tuple-element.6.basis, f32[64,256]{1,0:T(8,128)} %get-tuple-element.7.coeffs, f32[64,64]{1,0:T(8,128)} %get-tuple-element.8.spectrum), custom_call_target="tpu_custom_call" | custom-call | tf_op jit(solution)/shard_map/pallas_call | solution.py:471

commit v3 on v2

--- a/solution.py
+++ b/solution.py
@@ -13,14 +13,14 @@
 BF16 = jnp.bfloat16
 CHUNK = 2048
 HALF = CHUNK // 2
-SLOTS = 2
+SLOTS = 3
 PIECE = 128
 CUTS = 4
 PIECES = 4
 PHASES = 4
-LEAD = 3
-EARLY = 3
-LATE = 6
+LEAD = 4
+EARLY = 1
+LATE = 2
 PAIR = 1
 BACK = 1
 
@@ -52,11 +52,18 @@
     wide_line = lax.broadcasted_iota(jnp.int32, (k, 2 * k), 0)
     ident = jnp.where(line == lane, 1.0, 0.0).astype(F32)
     table = jnp.concatenate([gram, ident], axis=1)
-    for j in range(k - 1):
-        row = table[j : j + 1, :]
-        row = row / row[:, j : j + 1]
-        column = jnp.where(wide_line > j, table[:, j : j + 1], 0.0)
-        table = table - column * row
+    for j in range(0, k, 2):
+        column0 = jnp.broadcast_to(table[:, j : j + 1], (k, 2 * k))
+        column1 = jnp.broadcast_to(table[:, j + 1 : j + 2], (k, 2 * k))
+        pivot0 = column0[j : j + 1]
+        under = column0[j + 1 : j + 2]
+        beside = column1[j : j + 1] / pivot0
+        pivot1 = column1[j + 1 : j + 2] - under * beside
+        row0 = table[j : j + 1] / pivot0
+        row1 = (table[j + 1 : j + 2] - under * row0) / pivot1
+        column1 = jnp.where(wide_line > j + 1, column1 - column0 * beside, 0.0)
+        column0 = jnp.where(wide_line > j, column0, 0.0)
+        table = table - column0 * row0 - column1 * row1
     diag = jnp.sum(jnp.where(line == lane, table[:, :k], 0.0), axis=1, keepdims=True)
     return table[:, k:] / jnp.sqrt(diag)
 
@@ -71,8 +78,8 @@
     ranks, batch_total, scale,
     stress, sketch, basis_out, coeffs_out, spectrum_out,
     stage, high, low, operand, part, got1, summed, got2, panel,
-    acc, gacc, spread, landed, total, full, zone, lead, basis, spect, gram, grams, lead_factor,
-    stage_sem, basis_sem, send1, recv1, send2, recv2, send3, recv3,
+    acc, gacc, spread, landed, total, full, zone, lead, basis, held, sums, spectrum, spect, gram, grams, lead_factor,
+    stage_sem, small_sem, basis_sem, send1, recv1, send2, recv2, send3, recv3,
     rs_send, rs_recv, ag_send, ag_recv, sp_send, sp_recv, gr_send, gr_recv,
 ):
     groups = 4
@@ -99,7 +106,12 @@
             stage_sem.at[slot, q],
         )
 
-    for q in range(CUTS):
+    sketch_copy = pltpu.make_async_copy(sketch, held, small_sem.at[0])
+    coeffs_copy = pltpu.make_async_copy(sums, coeffs_out, small_sem.at[1])
+    spectrum_copy = pltpu.make_async_copy(spectrum, spectrum_out, small_sem.at[2])
+    load(0, 0).start()
+    sketch_copy.start()
+    for q in range(1, CUTS):
         load(0, q).start()
 
     barrier = pltpu.get_barrier_semaphore()
@@ -180,7 +192,7 @@
                 low[at, :] = l
                 return carry
 
-            lax.fori_loop(q * per_cut, (q + 1) * per_cut, body, 0)
+            lax.fori_loop(q * per_cut, (q + 1) * per_cut, body, 0, unroll=True)
 
     def project(p, c, h):
         at = pl.ds(c * CHUNK + h * HALF, HALF)
@@ -270,11 +282,11 @@
         operand[p, 0:kp, :] = h
         operand[p, kp:k, :] = l
 
-    for i in range(2):
-        set_operand(i, sketch[i * kp : (i + 1) * kp, :])
     acc[...] = jnp.zeros_like(acc)
     gacc[...] = jnp.zeros_like(gacc)
-    wait1, wait2 = EARLY * chunks // 16, LATE * chunks // 16
+    sketch_copy.wait()
+    for i in range(2):
+        set_operand(i, held[i * kp : (i + 1) * kp, :])
 
     def step(s, carry):
         @pl.when(s < units)
@@ -306,11 +318,11 @@
             fold_gram()
             reduce_start(done)
 
-        @pl.when(jnp.logical_and(live, at == wait1))
+        @pl.when(jnp.logical_and(live, at == EARLY))
         def _():
             reduce_share(done)
 
-        @pl.when(jnp.logical_and(live, at == wait2))
+        @pl.when(jnp.logical_and(live, at == LATE))
         def _():
             reduce_end(done)
 
@@ -341,11 +353,11 @@
 
     lax.fori_loop(0, units + PAIR + LEAD + BACK, step, 0)
 
+    reduce_start(3, width)
     fold_gram()
     own_gram = acc[:, width : width + k]
     gram[...] = own_gram
     grams[me_row] = own_gram
-    reduce_start(3, width)
     for d in range(1, ranks):
         give_gram(d).start()
     reduce_share(3, width)
@@ -358,15 +370,16 @@
     top = lead[...]
     f22 = inverse_factor(rest)
     low_top = dot_full(l21, top, 1, 0)
+    reduce_end(3, width)
+    found = jnp.concatenate([top, dot_full(f22, zone[:, 0:width] - low_top, 1, 0)], axis=0)
+    sums[...] = found
+    spect[0] = dot_full(found, found, 1, 1)
+    for d in range(1, groups):
+        share_spectrum(d).start()
+    coeffs_copy.start()
     for i, h, at in blocks:
         value = panel[3, me * per + i, h]
         basis[kp:k, at : at + HALF] = scale * value - dot_full(l21, basis[0:kp, at : at + HALF], 1, 0)
-    reduce_end(3, width)
-    sums = jnp.concatenate([top, dot_full(f22, zone[:, 0:width] - low_top, 1, 0)], axis=0)
-    coeffs_out[...] = sums
-    spect[0] = dot_full(sums, sums, 1, 1)
-    for d in range(1, groups):
-        share_spectrum(d).start()
     for i, h, at in blocks:
         basis[kp:k, at : at + HALF] = dot_full(f22, basis[kp:k, at : at + HALF], 1, 0)
     basis_copy(1).start()
@@ -376,9 +389,12 @@
         share_spectrum(d).wait()
     a = spect[0] + spect[2]
     b = spect[1] + spect[3]
-    spectrum_out[...] = (a + b) / batch_total
+    spectrum[...] = (a + b) / batch_total
+    spectrum_copy.start()
+    coeffs_copy.wait()
     for i in range(2):
         basis_copy(i).wait()
+    spectrum_copy.wait()
 
 
 def finish(basis, coeffs, spectrum, basis_out, coeffs_out, spectrum_out, hold, rows, tiny, came, went):
@@ -409,7 +425,7 @@
     lines = kp // ranks
     wide = width + 128
     scale = math.sqrt(float(rows_dev * ranks))
-    vmem = pl.BlockSpec(memory_space=pltpu.VMEM)
+    anywhere = pl.BlockSpec(memory_space=pl.ANY)
     dma = pltpu.SemaphoreType.DMA
     found = pl.pallas_call(
         functools.partial(kernel, ranks, float(width * groups), scale),
@@ -418,8 +434,8 @@
             jax.ShapeDtypeStruct((k, width), F32),
             jax.ShapeDtypeStruct((k, k), F32),
         ),
-        in_specs=[pl.BlockSpec(memory_space=pl.ANY), vmem],
-        out_specs=(pl.BlockSpec(memory_space=pl.ANY), vmem, vmem),
+        in_specs=[anywhere] * 2,
+        out_specs=(anywhere,) * 3,
         scratch_shapes=[
             pltpu.VMEM((SLOTS, CHUNK, width), F32),
             pltpu.VMEM((rows_dev, width), BF16),
@@ -439,11 +455,15 @@
             pltpu.VMEM((kp, wide), F32),
             pltpu.VMEM((kp, width), F32),
             pltpu.VMEM((k, share), F32),
+            pltpu.VMEM((k, width), F32),
+            pltpu.VMEM((k, width), F32),
+            pltpu.VMEM((k, k), F32),
             pltpu.VMEM((groups, k, k), F32),
             pltpu.VMEM((kp, k), F32),
             pltpu.VMEM((ranks, kp, k), F32),
             pltpu.VMEM((kp, kp), F32),
             dma((SLOTS, CUTS)),
+            dma((3,)),
             dma((2,)),
             dma((PHASES, chunks)),
             dma((PHASES, chunks)),
@@ -467,7 +487,6 @@
             flops=24 * rows_dev * width * k, bytes_accessed=rows_dev * width * 4, transcendentals=0
         ),
     )(stress, sketch)
-    anywhere = pl.BlockSpec(memory_space=pl.ANY)
     return pl.pallas_call(
         finish,
         out_shape=tuple(jax.ShapeDtypeStruct(a.shape, a.dtype) for a in found),

time: 120 us -> 120 us (level)
  no operation moved by 1% of the time
where the time goes in v3:
time: 120 us; the launch traced here: 119 us
  Pallas kernels  119 us (99%)
    pallas_call x1, Pallas kernels, on_device(): pl.pallas_call(functools.partial(kernel, ranks, float(width * groups), sc...  117 us

profile of v3, /device:TPU:0, one launch (start us, length us, event | category | flops | bytes accessed | tf_op | source)
XLA Modules:
  0.0 119.2 jit_solution(16305861955397336337)
XLA Ops:
  0.6 116.5 %shard_map.49 = (f32[64,4096]{1,0:T(8,128)}, f32[64,256]{1,0:T(8,128)}, f32[64,64]{1,0:T(8,128)}) custom-call(f32[16384,256]{1,0:T(8,128)} %stress.1, f32[64,256]{1,0:T(8,128)} %sketch.1), custom_call_target="tpu_custom_call" | custom-call | flops 6442450944 | bytes 16777216 | tf_op jit(solution)/shard_map/pallas_call | solution.py:430
  117.2 2.1 %shard_map.50 = (f32[64,4096]{1,0:T(8,128)}, f32[64,256]{1,0:T(8,128)}, f32[64,64]{1,0:T(8,128)}) custom-call(f32[64,4096]{1,0:T(8,128)} %get-tuple-element.6.basis, f32[64,256]{1,0:T(8,128)} %get-tuple-element.7.coeffs, f32[64,64]{1,0:T(8,128)} %get-tuple-element.8.spectrum), custom_call_target="tpu_custom_call" | custom-call | tf_op jit(solution)/shard_map/pallas_call | solution.py:490

commit v4 on v3

--- a/solution.py
+++ b/solution.py
@@ -16,7 +16,7 @@
 SLOTS = 3
 PIECE = 128
 CUTS = 4
-PIECES = 4
+PIECES = 2
 PHASES = 4
 LEAD = 4
 EARLY = 1
@@ -224,15 +224,13 @@
         panel[p, c, mine] = summed[c] + got2[p, c]
         hop3(p, c).start()
 
-    def stacked(p, c):
-        value = jnp.concatenate([panel[p, c, 0], panel[p, c, 1]], axis=1)
-        hi, lo = split(value)
+    def stacked(p, c, h):
+        hi, lo = split(panel[p, c, h])
         return jnp.concatenate([hi, lo], axis=0)
 
-    def accumulate(p, c):
-        hop3(p, c).wait()
-        stack = stacked(p, c)
-        at = pl.ds(c * CHUNK, CHUNK)
+    def accumulate(p, c, h):
+        stack = stacked(p, c, h)
+        at = pl.ds(c * CHUNK + h * HALF, HALF)
         both = dot(stack, high[at, :], 1, 0)
         rest = dot(stack[0:kp], low[at, :], 1, 0)
         acc[:, 0:width] += both[0:kp] + (both[kp:k] + rest)
@@ -243,7 +241,7 @@
 
         @pl.when(p % 2 == 1)
         def _():
-            gacc[...] += dot(stack, jnp.concatenate([stacked(p - 1, c), stack], axis=0), 1, 1)
+            gacc[...] += dot(stack, jnp.concatenate([stacked(p - 1, c, h), stack], axis=0), 1, 1)
 
     def fold_gram():
         rows = gacc[0:kp, :] + gacc[kp:k, :]
@@ -306,7 +304,9 @@
         @pl.when(s >= PAIR + LEAD + BACK)
         def _():
             u = s - PAIR - LEAD - BACK
-            accumulate(u // chunks, u % chunks)
+            p, c = u // chunks, u % chunks
+            hop3(p, c).wait()
+            accumulate(p, c, 1 - mine)
 
         since = s - (chunks - 1 + PAIR + LEAD + BACK)
         done = since // chunks
@@ -348,6 +348,11 @@
                     value = panel[2, me * per + i, h]
                     basis[0:kp, at : at + HALF] = dot_full(scaled, value, 1, 0)
                 basis_copy(0).start()
+
+        @pl.when(jnp.logical_and(s >= PAIR + LEAD, s < units + PAIR + LEAD))
+        def _():
+            u = s - PAIR - LEAD
+            accumulate(u // chunks, u % chunks, mine)
 
         return carry
 

time: 120 us -> 119 us (level)
  no operation moved by 1% of the time
where the time goes in v4:
time: 119 us
  Pallas kernels  118 us (99%)
    pallas_call x1, Pallas kernels, on_device(): pl.pallas_call(functools.partial(kernel, ranks, float(width * groups), sc...  116 us

profile of v4, /device:TPU:0, one launch (start us, length us, event | category | flops | bytes accessed | tf_op | source)
XLA Modules:
  0.0 119.0 jit_solution(16024202411091785417)
XLA Ops:
  0.6 116.3 %shard_map.49 = (f32[64,4096]{1,0:T(8,128)}, f32[64,256]{1,0:T(8,128)}, f32[64,64]{1,0:T(8,128)}) custom-call(f32[16384,256]{1,0:T(8,128)} %stress.1, f32[64,256]{1,0:T(8,128)} %sketch.1), custom_call_target="tpu_custom_call" | custom-call | flops 6442450944 | bytes 16777216 | tf_op jit(solution)/shard_map/pallas_call | solution.py:435
  116.9 2.1 %shard_map.50 = (f32[64,4096]{1,0:T(8,128)}, f32[64,256]{1,0:T(8,128)}, f32[64,64]{1,0:T(8,128)}) custom-call(f32[64,4096]{1,0:T(8,128)} %get-tuple-element.6.basis, f32[64,256]{1,0:T(8,128)} %get-tuple-element.7.coeffs, f32[64,64]{1,0:T(8,128)} %get-tuple-element.8.spectrum), custom_call_target="tpu_custom_call" | custom-call | tf_op jit(solution)/shard_map/pallas_call | solution.py:495

commit v5 on v4

--- a/solution.py
+++ b/solution.py
@@ -378,7 +378,10 @@
     reduce_end(3, width)
     found = jnp.concatenate([top, dot_full(f22, zone[:, 0:width] - low_top, 1, 0)], axis=0)
     sums[...] = found
-    spect[0] = dot_full(found, found, 1, 1)
+    stack = jnp.concatenate(split(found), axis=0)
+    both = dot(stack, stack, 1, 1)
+    rows = both[0:k] + both[k : 2 * k]
+    spect[0] = rows[:, 0:k] + rows[:, k : 2 * k]
     for d in range(1, groups):
         share_spectrum(d).start()
     coeffs_copy.start()

time: 119 us -> 119 us (level)
  no operation moved by 1% of the time
where the time goes in v5:
time: 119 us
  Pallas kernels  118 us (99%)
    pallas_call x1, Pallas kernels, on_device(): pl.pallas_call(functools.partial(kernel, ranks, float(width * groups), sc...  116 us

profile of v5, /device:TPU:0, one launch (start us, length us, event | category | flops | bytes accessed | tf_op | source)
XLA Modules:
  0.0 119.1 jit_solution(5360069222611550028)
XLA Ops:
  0.6 116.3 %shard_map.49 = (f32[64,4096]{1,0:T(8,128)}, f32[64,256]{1,0:T(8,128)}, f32[64,64]{1,0:T(8,128)}) custom-call(f32[16384,256]{1,0:T(8,128)} %stress.1, f32[64,256]{1,0:T(8,128)} %sketch.1), custom_call_target="tpu_custom_call" | custom-call | flops 6442450944 | bytes 16777216 | tf_op jit(solution)/shard_map/pallas_call | solution.py:438
  116.9 2.1 %shard_map.50 = (f32[64,4096]{1,0:T(8,128)}, f32[64,256]{1,0:T(8,128)}, f32[64,64]{1,0:T(8,128)}) custom-call(f32[64,4096]{1,0:T(8,128)} %get-tuple-element.6.basis, f32[64,256]{1,0:T(8,128)} %get-tuple-element.7.coeffs, f32[64,64]{1,0:T(8,128)} %get-tuple-element.8.spectrum), custom_call_target="tpu_custom_call" | custom-call | tf_op jit(solution)/shard_map/pallas_call | solution.py:498
